TPU v7x, 512 devices: a whole 4x4x16 slice. The times are simulated.
512 devices in a mesh: row: 16 (over x, y_lo, core), col: 32 (over z, y_hi).
Axes of the slice: x: 4, y: 4 (y_hi: 2, y_lo: 2; y = y_hi * 2 + y_lo), z: 16, core: 2. Of those that a mesh axis runs over, the one named last changes fastest.
Arguments:
- features: bfloat16 [128, 1024, 256], P('row', 'col'), may hold values from -16 to 16
- expand_weight: bfloat16 [2, 256, 1024], replicated, may hold values from -0.375 to 0.375
- expand_bias: float32 [2, 1024], replicated, may hold values from -3 to 3
- depth_weight: float32 [2, 3, 3, 1024], replicated, may hold values from -2 to 2
- depth_bias: float32 [2, 1024], replicated, may hold values from -3 to 3
- project_weight: bfloat16 [2, 1024, 256], replicated, may hold values from -0.1875 to 0.1875
- project_bias: float32 [2, 256], replicated, may hold values from -3 to 3
- qkv_weight: bfloat16 [2, 256, 768], replicated, may hold values from -0.375 to 0.375
- aggregate_depth: float32 [2, 5, 5, 768], replicated, may hold values from -1.25 to 1.25
- aggregate_group: bfloat16 [2, 24, 32, 32], replicated, may hold values from -1 to 1
- output_weight: bfloat16 [2, 512, 256], replicated, may hold values from -0.25 to 0.25
- output_bias: float32 [2, 256], replicated, may hold values from -3 to 3
- head_weight: bfloat16 [3, 3, 4, 256], replicated, may hold values from -0.125 to 0.125
- head_bias: float32 [4], replicated, may hold values from -3 to 3
Outputs:
- final_map: bfloat16 [128, 1024, 256], P('row', 'col')
- boxes: float32 [4, 128, 1024], P(None, 'row', 'col')
All inputs are finite; a program needn't handle non-finite values.
Results may differ from a plain program's by a relative error of at most 0.009.
Values may be sent and summed in bfloat16 or wider, within the bound.
A program may use at most 64 MiB of HBM per device.

v0:
```python
import jax
import jax.numpy as jnp
from jax import lax
from jax.sharding import PartitionSpec as P

SECTIONS = 2


def with_halo(cells, sides, width):
    for axis, dim in sides:
        count = lax.axis_size(axis)
        ends = count - 1
        head = lax.slice_in_dim(cells, 0, width, axis=dim)
        tail = lax.slice_in_dim(cells, cells.shape[dim] - width, cells.shape[dim], axis=dim)
        cells = jnp.concatenate(
            [
                lax.ppermute(tail, axis, [(i, (i + 1) % count) for i in range(ends)]),
                cells,
                lax.ppermute(head, axis, [((i + 1) % count, i) for i in range(ends)]),
            ],
            axis=dim,
        )
    return cells


def hard_swish(value):
    return value * jnp.minimum(jnp.maximum(value + 3.0, 0.0), 6.0) / 6.0


def depthwise(padded, weight, rows, cols):
    ksize = weight.shape[0]
    total = jnp.zeros((rows, cols, padded.shape[2]), jnp.float32)
    for offset_r in range(ksize):
        for offset_c in range(ksize):
            total = (
                total
                + padded[offset_r : offset_r + rows, offset_c : offset_c + cols, :].astype(
                    jnp.float32
                )
                * weight[offset_r, offset_c]
            )
    return total


def dense(values, weight):
    return lax.dot_general(
        values, weight, (((values.ndim - 1,), (0,)), ((), ())), preferred_element_type=jnp.float32
    )


def heads_of(padded_qkv, agg_depth, agg_group, rows, cols, heads, head_dim):
    center = padded_qkv[2 : 2 + rows, 2 : 2 + cols, :]
    spread = depthwise(padded_qkv, agg_depth, rows, cols).astype(jnp.bfloat16)
    grouped = jnp.einsum(
        "rcgd,gde->rcge",
        spread.reshape(rows, cols, 3 * heads, head_dim),
        agg_group,
        preferred_element_type=jnp.float32,
    ).astype(jnp.bfloat16)
    return jnp.concatenate(
        [
            center.reshape(rows, cols, heads, 3, head_dim),
            grouped.reshape(rows, cols, heads, 3, head_dim),
        ],
        axis=2,
    )


def local(
    features,
    expand_weight,
    expand_bias,
    depth_weight,
    depth_bias,
    project_weight,
    project_bias,
    qkv_weight,
    aggregate_depth,
    aggregate_group,
    output_weight,
    output_bias,
    head_weight,
    head_bias,
):
    rows, cols, width = features.shape
    head_dim = aggregate_group.shape[2]
    heads = width // head_dim
    current = features
    for section in range(SECTIONS):
        hidden = hard_swish(dense(current, expand_weight[section]) + expand_bias[section]).astype(
            jnp.bfloat16
        )
        hidden = with_halo(hidden, (("row", 0), ("col", 1)), 1)
        spread = hard_swish(
            depthwise(hidden, depth_weight[section], rows, cols) + depth_bias[section]
        ).astype(jnp.bfloat16)
        mixed = (current + dense(spread, project_weight[section]) + project_bias[section]).astype(
            jnp.bfloat16
        )
        local_qkv = dense(mixed, qkv_weight[section]).astype(jnp.bfloat16)
        padded_qkv = with_halo(local_qkv, (("row", 0), ("col", 1)), 2)
        both = heads_of(
            padded_qkv,
            aggregate_depth[section],
            aggregate_group[section],
            rows,
            cols,
            heads,
            head_dim,
        )
        queries = jax.nn.relu(both[:, :, :, 0, :]).astype(jnp.float32)
        keys = jax.nn.relu(both[:, :, :, 1, :]).astype(jnp.float32)
        values = both[:, :, :, 2, :].astype(jnp.float32)
        kv_local = jnp.einsum("rchd,rche->hde", keys, values, precision=lax.Precision.HIGHEST)
        key_local = jnp.sum(keys, axis=(0, 1))
        kv_all, key_all = lax.psum((kv_local, key_local), ("row", "col"))
        numer = jnp.einsum("rchd,hde->rche", queries, kv_all, precision=lax.Precision.HIGHEST)
        denom = jnp.einsum("rchd,hd->rch", queries, key_all, precision=lax.Precision.HIGHEST)
        attended = (
            (numer / (denom[..., None] + 1e-06)).astype(jnp.bfloat16).reshape(rows, cols, 2 * width)
        )
        current = (mixed + dense(attended, output_weight[section]) + output_bias[section]).astype(
            jnp.bfloat16
        )
    padded = with_halo(current, (("row", 0), ("col", 1)), 1)
    boxes = jnp.zeros((4, rows, cols), jnp.float32)
    for offset_r in range(3):
        for offset_c in range(3):
            window = padded[offset_r : offset_r + rows, offset_c : offset_c + cols, :]
            boxes = boxes + lax.dot_general(
                head_weight[offset_r, offset_c],
                window,
                (((1,), (2,)), ((), ())),
                preferred_element_type=jnp.float32,
            )
    boxes = boxes + head_bias[:, None, None]
    return (current, boxes)


def solution(mesh):
    return jax.shard_map(
        local,
        mesh=mesh,
        in_specs=(
            P("row", "col", None),
            P(),
            P(),
            P(),
            P(),
            P(),
            P(),
            P(),
            P(),
            P(),
            P(),
            P(),
            P(),
            P(),
        ),
        out_specs=(P("row", "col", None), P(None, "row", "col")),
        check_vma=False,
    )
```

profile of v0, /device:TPU:1, one launch (start us, length us, event | category | flops | bytes accessed | tf_op | source)
XLA Modules:
  0.0 1291.3 jit_solution(16654592046291332820)
XLA Ops:
  7.3 1.4 fusion.129
  8.6 1.5 multiply_convert_fusion.3
  10.1 4.6 collective-permute-start
  14.7 5.5 collective-permute-start.1
  21.7 0.7 copy_bitcast_fusion
  23.1 1.9 collective-permute-start.2
  24.9 1.3 collective-permute-start.3
  26.2 0.7 slice_reduce_fusion.49
  27.0 4.2 collective-permute-done.3
  31.6 1.5 fusion.11
  33.4 0.7 fusion.122
  34.1 3.7 collective-permute-start.4
  37.8 1.9 collective-permute-start.5
  39.7 0.6 slice_reduce_fusion.48
  40.4 1.6 reshape.49
  42.0 2.0 collective-permute-done.5
  44.0 6.0 collective-permute-start.6
  50.0 1.3 collective-permute-start.7
  51.3 1.9 copy_dynamic-update-slice_fusion.3
  53.3 2.9 collective-permute-done.7
  56.7 3.0 add_convert_fusion.1
  59.7 1.1 reshape.50
  61.3 1.3 copy-done
  63.4 1.4 copy-done.1
  64.8 1.1 convolution_bitcast_fusion.1
  66.0 111.1 %psum.29 = f32[16,32]{1,0:T(8,128)S(1)} all-reduce(f32[16,32]{1,0:T(8,128)S(1)} %convert_reduce_fusion.1), channel_id=1, replica_groups=mesh['row'=16,'col'=32] {'row','col'}, use_global_device_ids=true, to_apply=%region_2.3 | all-reduce | flops 512 | bytes 4096 | tf_op jit(solution)/shard_map/psum | solution.py:116
  177.0 5.4 fusion.26
  182.5 450.1 %all-reduce.3.cloned.1.call-done = f32[16,32,32]{1,2,0:T(8,128)} async-done(((f32[16,32,32]{1,2,0:T(8,128)}), f32[16,32,32]{1,2,0:T(8,128)}) %all-reduce.3.cloned.1.call-update) | async-done | bytes 65552 | tf_op jit(solution)/shard_map/psum | solution.py:116
  632.6 6.1 fusion.1
  638.7 1.0 copy.25
  639.7 1.0 reshape.52
  640.8 1.2 fusion.8
  642.4 4.9 collective-permute-start.8
  647.3 1.9 collective-permute-start.9
  649.3 3.6 collective-permute-done.9
  653.0 4.5 collective-permute-start.10
  657.5 1.3 collective-permute-start.11
  658.9 4.8 collective-permute-done.11
  664.1 1.5 fusion.10
  666.0 2.7 collective-permute-start.12
  668.7 1.9 collective-permute-start.13
  670.7 1.6 reshape.53
  672.3 2.3 collective-permute-done.13
  674.7 3.1 collective-permute-start.14
  677.8 1.5 collective-permute-start.15
  679.3 1.9 copy_dynamic-update-slice_fusion.1
  681.2 2.8 collective-permute-done.15
  684.3 3.0 add_convert_fusion
  687.3 1.1 reshape.54
  689.0 1.3 copy-done.2
  691.1 1.4 copy-done.3
  692.4 1.1 convolution_bitcast_fusion
  693.6 105.8 %psum.31 = f32[16,32]{1,0:T(8,128)S(1)} all-reduce(f32[16,32]{1,0:T(8,128)S(1)} %convert_reduce_fusion), channel_id=1, replica_groups=mesh['row'=16,'col'=32] {'row','col'}, use_global_device_ids=true, to_apply=%region_5.6 | all-reduce | flops 512 | bytes 4096 | tf_op jit(solution)/shard_map/psum | solution.py:116
  799.4 5.4 fusion.29
  804.9 448.7 %all-reduce.5.cloned.1.call-done = f32[16,32,32]{1,2,0:T(8,128)} async-done(((f32[16,32,32]{1,2,0:T(8,128)}), f32[16,32,32]{1,2,0:T(8,128)}) %all-reduce.5.cloned.1.call-update) | async-done | bytes 65552 | tf_op jit(solution)/shard_map/psum | solution.py:116
  1253.6 6.1 fusion
  1259.8 1.0 copy.31
  1260.8 1.0 reshape.56
  1262.1 4.9 collective-permute-start.16
  1267.0 1.9 collective-permute-start.17
  1269.2 2.9 collective-permute-done.17
  1272.1 4.5 collective-permute-start.18
  1276.6 1.3 collective-permute-start.19
  1278.3 4.2 collective-permute-done.19
  (151 shorter events, 10.5 us)
Async XLA Ops:
  7.2 13.1 %copy-start.35 = (f32[2,256]{1,0:T(2,128)S(1)}, f32[2,256]{1,0:T(2,128)}, u32[]{:S(2)}) copy-start(f32[2,256]{1,0:T(2,128)} %param.20) | copy-start | bytes 6148
  7.2 13.7 %copy-start.32 = (f32[2,1024]{1,0:T(2,128)S(1)}, f32[2,1024]{1,0:T(2,128)}, u32[]{:S(2)}) copy-start(f32[2,1024]{1,0:T(2,128)} %param.18) | copy-start | bytes 24580
  7.2 14.3 %copy-start.14 = (f32[2,3,3,1024]{3,0,2,1:T(2,128)S(1)}, f32[2,3,3,1024]{3,0,2,1:T(2,128)}, u32[]{:S(2)}) copy-start(f32[2,3,3,1024]{3,0,2,1:T(2,128)} %param.17) | copy-start | bytes 221188
  7.2 14.4 %copy-start.9 = (f32[2,5,5,768]{3,0,2,1:T(2,128)S(1)}, f32[2,5,5,768]{3,0,2,1:T(2,128)}, u32[]{:S(2)}) copy-start(f32[2,5,5,768]{3,0,2,1:T(2,128)} %param.22) | copy-start | bytes 460804
  7.2 625.4 %all-reduce.3.cloned.1.call-start = ((), (), s32[]{:S(2)}) async-start(), calls=%async_computation | async-start | bytes 524288 | tf_op jit(solution)/shard_map/psum | solution.py:116
  8.6 13.8 %copy-start.36 = (f32[2,256]{1,0:T(2,128)S(1)}, f32[2,256]{1,0:T(2,128)}, u32[]{:S(2)}) copy-start(f32[2,256]{1,0:T(2,128)} %param.25) | copy-start | bytes 6148
  10.1 12.8 collective-permute-start
  14.7 8.2 collective-permute-start.1
  23.0 8.6 copy-start.42
  23.0 8.6 copy-start.45
  23.1 3.9 collective-permute-start.2
  24.9 6.3 collective-permute-start.3
  33.1 6.6 copy-start.10
  34.1 7.9 collective-permute-start.4
  37.8 6.1 collective-permute-start.5
  44.0 9.3 collective-permute-start.6
  50.0 6.2 collective-permute-start.7
  53.2 3.3 copy-start.15
  53.2 3.3 copy-start.16
  53.2 3.3 copy-start.17
  53.2 3.4 copy-start.18
  53.2 3.4 copy-start.19
  53.2 3.4 copy-start.20
  53.2 3.4 copy-start.21
  53.2 3.4 copy-start.22
  53.2 3.4 copy-start.23
  53.2 3.4 copy-start.24
  53.3 3.4 copy-start.25
  53.3 3.4 copy-start.26
  53.3 3.4 copy-start.27
  53.3 3.4 copy-start.28
  53.3 3.4 copy-start.29
  53.3 3.4 copy-start.30
  53.3 3.4 copy-start.31
  60.8 1.9 copy-start
  182.4 1071.2 %all-reduce.5.cloned.1.call-start = ((), (), s32[]{:S(2)}) async-start(), calls=%async_computation.1 | async-start | bytes 524288 | tf_op jit(solution)/shard_map/psum | solution.py:116
  638.7 2.0 copy-start.11
  638.7 2.0 copy-start.39
  638.7 3.2 copy-start.34
  639.7 2.2 copy-start.41
  642.0 16.8 %copy-start.8 = (f32[5,5,768]{2,1,0:T(8,128)S(1)}, f32[5,5,768]{2,1,0:T(8,128)}, u32[]{:S(2)}) copy-start(f32[5,5,768]{2,1,0:T(8,128)} %get-tuple-element.118) | copy-start | bytes 230404
  642.4 7.0 collective-permute-start.8
  647.3 5.6 collective-permute-start.9
  649.3 14.8 %copy-start.33 = (f32[1,1024]{1,0:T(1,128)S(1)}, f32[1,1024]{1,0:T(1,128)}, u32[]{:S(2)}) copy-start(f32[1,1024]{1,0:T(1,128)} %get-tuple-element.108) | copy-start | bytes 12292
  649.3 14.8 %copy-start.38 = (f32[1,256]{1,0:T(1,128)S(1)}, f32[1,256]{1,0:T(1,128)}, u32[]{:S(2)}) copy-start(f32[1,256]{1,0:T(1,128)} %get-tuple-element.114) | copy-start | bytes 3076
  649.3 14.8 %copy-start.43 = (bf16[2,1024,256]{2,1,0:T(8,128)(2,1)S(1)}, bf16[2,1024,256]{2,1,0:T(8,128)(2,1)}, u32[]{:S(2)}) copy-start(bf16[2,1024,256]{2,1,0:T(8,128)(2,1)} %param.19) | copy-start | bytes 3145732
  653.0 6.0 collective-permute-start.10
  657.5 6.3 collective-permute-start.11
  665.6 5.0 copy-start.12
  666.0 6.3 collective-permute-start.12
  668.7 5.9 collective-permute-start.13
  674.7 6.6 collective-permute-start.14
  677.8 6.2 collective-permute-start.15
  688.4 1.9 copy-start.2
  1259.7 2.0 copy-start.13
  1259.8 2.0 copy-start.37
  1259.8 2.0 copy-start.44
  1259.8 9.2 copy-start.40
  1261.8 21.8 %copy-start.46 = (f32[4]{0:T(128)S(1)}, f32[4]{0:T(128)}, u32[]{:S(2)}) copy-start(f32[4]{0:T(128)} %param.27) | copy-start | bytes 52
  1262.0 22.4 %copy-start.4 = (bf16[8,32,256]{2,1,0:T(8,128)(2,1)}, bf16[8,32,256]{2,1,0:T(8,128)(2,1)S(1)}, u32[]{:S(2)}) copy-start(bf16[8,32,256]{2,1,0:T(8,128)(2,1)S(1)} %fusion.9) | copy-start | bytes 393220
  1262.1 7.1 collective-permute-start.16
  1267.0 5.1 collective-permute-start.17
  1272.1 6.2 collective-permute-start.18
  1276.6 5.9 collective-permute-start.19
  (5 other events, 7.0 us)
Sparse Core Ops, SparseCore 0:
  182.6 449.9 all-reduce.2
  805.0 448.5 all-reduce.4
where the time goes:
time: 1290 us
  waiting for transfers between devices  929 us (72%)
  blocking collectives  217 us (17%)
  starting transfers between devices  60.7 us (5%)
  matrix products  35 us (3%)
  local copies, waits for them, and re-layouts  26.6 us (2%)
  between operations  15.2 us (1%)
    psum x2, waiting for transfers between devices, local(): kv_all, key_all = lax.psum((kv_local, key_local), ('row', 'col'))  899 us
    psum x2, blocking collectives, local(): kv_all, key_all = lax.psum((kv_local, key_local), ('row', 'col'))  217 us
    ppermute x10, starting transfers between devices, with_halo(): lax.ppermute(tail, axis, [(i, (i + 1) % count) for i in range(ends)])  40.8 us
    ppermute x10, waiting for transfers between devices, with_halo(): lax.ppermute(head, axis, [((i + 1) % count, i) for i in range(ends)])  29.7 us
  transfers between devices with their start and end apart: 22, of which 11 were waited for; matrix products, arithmetic and copies ran while one was open for 1% of the time, Pallas kernels for 0%

commit v1 on v0

--- a/solution.py
+++ b/solution.py
@@ -113,7 +113,7 @@
         values = both[:, :, :, 2, :].astype(jnp.float32)
         kv_local = jnp.einsum("rchd,rche->hde", keys, values, precision=lax.Precision.HIGHEST)
         key_local = jnp.sum(keys, axis=(0, 1))
-        kv_all, key_all = lax.psum((kv_local, key_local), ("row", "col"))
+        kv_all, key_all = lax.psum(lax.psum((kv_local, key_local), "row"), "col")
         numer = jnp.einsum("rchd,hde->rche", queries, kv_all, precision=lax.Precision.HIGHEST)
         denom = jnp.einsum("rchd,hd->rch", queries, key_all, precision=lax.Precision.HIGHEST)
         attended = (

time: 1290 us -> 1250 us (0.969)
  waiting for transfers between devices: 929 us -> 885 us
  starting transfers between devices: 60.7 us -> 95.9 us
  blocking collectives: 217 us -> 183 us
    psum x2 -> x4, waiting for transfers between devices: 899 us -> 855 us  [local(): kv_all, key_all = lax.psum(lax.psum((kv_local, key_local), 'row'), 'col')]
    ppermute x10, starting transfers between devices: 40.8 us -> 75.5 us  [with_halo(): lax.ppermute(tail, axis, [(i, (i + 1) % count) for i in range(ends)])]
    psum x2 -> x4, blocking collectives: 217 us -> 183 us  [local(): kv_all, key_all = lax.psum(lax.psum((kv_local, key_local), 'row'), 'col')]
  transfers between devices with their start and end apart: 22 -> 24, of which waited for: 11 -> 13; matrix products, arithmetic and copies ran while one was open for 1% -> 2% of each run, Pallas kernels for 0% -> 0%
where the time goes in v1:
time: 1250 us
  waiting for transfers between devices  885 us (71%)
  blocking collectives  183 us (15%)
  starting transfers between devices  95.9 us (8%)
  matrix products  35 us (3%)
  local copies, waits for them, and re-layouts  26.6 us (2%)
  between operations  15 us (1%)
    psum x4, waiting for transfers between devices, local(): kv_all, key_all = lax.psum(lax.psum((kv_local, key_local), 'row'), 'col')  855 us
    psum x4, blocking collectives, local(): kv_all, key_all = lax.psum(lax.psum((kv_local, key_local), 'row'), 'col')  183 us
    ppermute x10, starting transfers between devices, with_halo(): lax.ppermute(tail, axis, [(i, (i + 1) % count) for i in range(ends)])  75.5 us
    ppermute x10, waiting for transfers between devices, with_halo(): lax.ppermute(head, axis, [((i + 1) % count, i) for i in range(ends)])  29.7 us
  transfers between devices with their start and end apart: 24, of which 13 were waited for; matrix products, arithmetic and copies ran while one was open for 2% of the time, Pallas kernels for 0%

profile of v1, /device:TPU:1, one launch (start us, length us, event | category | flops | bytes accessed | tf_op | source)
XLA Modules:
  0.0 1248.6 jit_solution(2628014274538968885)
XLA Ops:
  7.3 1.4 fusion.129
  8.6 1.5 multiply_convert_fusion.3
  10.1 4.6 collective-permute-start
  14.7 5.5 collective-permute-start.1
  23.1 1.9 collective-permute-start.2
  24.9 1.3 collective-permute-start.3
  27.0 4.2 collective-permute-done.3
  31.6 1.5 fusion.11
  34.1 3.7 collective-permute-start.4
  37.8 1.9 collective-permute-start.5
  40.4 1.6 reshape.49
  42.0 2.0 collective-permute-done.5
  44.0 6.0 collective-permute-start.6
  50.0 1.3 collective-permute-start.7
  51.3 1.9 copy_dynamic-update-slice_fusion.3
  53.3 2.9 collective-permute-done.7
  56.7 3.0 add_convert_fusion.1
  59.7 1.1 reshape.50
  61.3 1.3 copy-done
  63.4 1.4 copy-done.1
  64.8 1.1 convolution_bitcast_fusion.1
  66.0 26.4 %psum.58 = f32[16,32]{1,0:T(8,128)S(1)} all-reduce(f32[16,32]{1,0:T(8,128)S(1)} %convert_reduce_fusion.1), channel_id=1, replica_groups=mesh['row'=16,'col'=32] {'row'}, use_global_device_ids=true, to_apply=%region_3.4 | all-reduce | flops 512 | bytes 4096 | tf_op jit(solution)/shard_map/psum | solution.py:116
  92.3 68.7 %psum.59 = f32[16,32]{1,0:T(8,128)S(1)} all-reduce(f32[16,32]{1,0:T(8,128)S(1)} %psum.58), channel_id=1, replica_groups=mesh['row'=16,'col'=32] {'col'}, use_global_device_ids=true, to_apply=%region_4.5 | all-reduce | flops 512 | bytes 4096 | tf_op jit(solution)/shard_map/psum | solution.py:116
  161.3 5.4 fusion.26
  166.7 136.4 %all-reduce.5.cloned.1.call-done = f32[16,32,32]{1,2,0:T(8,128)} async-done(((f32[16,32,32]{1,2,0:T(8,128)}), f32[16,32,32]{1,2,0:T(8,128)}) %all-reduce.5.cloned.1.call-update) | async-done | bytes 65552 | tf_op jit(solution)/shard_map/psum | solution.py:116
  303.1 290.3 %all-reduce.7.cloned.1.call-done = f32[16,32,32]{1,2,0:T(8,128)} async-done(((f32[16,32,32]{1,2,0:T(8,128)}), f32[16,32,32]{1,2,0:T(8,128)}) %all-reduce.7.cloned.1.call-update) | async-done | bytes 65552 | tf_op jit(solution)/shard_map/psum | solution.py:116
  593.4 6.1 fusion.1
  599.6 1.0 copy.25
  600.6 1.0 reshape.52
  601.6 1.2 fusion.8
  603.2 22.5 %collective-permute-start.8 = (bf16[1,32,1024]{2,1,0:T(8,128)(2,1)S(1)}, bf16[1,32,1024]{2,1,0:T(8,128)(2,1)S(1)}, u32[]{:S(2)}, u32[]{:S(2)}) collective-permute-start(bf16[1,32,1024]{2,1,0:T(8,128)(2,1)S(1)} %get-tuple-element.72), channel_id=1, source_target_pairs={{0,32},{32,64},{64,96},{96,128},{128,160},{160,192},{192,224},{224... | collective-permute-start | bytes 196616 | tf_op jit(solution)/shard_map/ppermute | solution.py:17
  625.7 1.9 collective-permute-start.9
  627.7 3.6 collective-permute-done.9
  631.4 3.1 collective-permute-start.10
  634.4 1.3 collective-permute-start.11
  635.9 4.8 collective-permute-done.11
  641.1 1.5 fusion.10
  642.9 2.7 collective-permute-start.12
  645.6 1.9 collective-permute-start.13
  647.6 1.6 reshape.53
  649.2 2.3 collective-permute-done.13
  651.6 5.5 collective-permute-start.14
  657.1 1.5 collective-permute-start.15
  658.7 1.9 copy_dynamic-update-slice_fusion.1
  660.5 2.8 collective-permute-done.15
  663.7 3.0 add_convert_fusion
  666.7 1.1 reshape.54
  668.3 1.3 copy-done.2
  670.4 1.4 copy-done.3
  671.8 1.1 convolution_bitcast_fusion
  672.9 26.3 %psum.62 = f32[16,32]{1,0:T(8,128)S(1)} all-reduce(f32[16,32]{1,0:T(8,128)S(1)} %convert_reduce_fusion), channel_id=1, replica_groups=mesh['row'=16,'col'=32] {'row'}, use_global_device_ids=true, to_apply=%region_8.9 | all-reduce | flops 512 | bytes 4096 | tf_op jit(solution)/shard_map/psum | solution.py:116
  699.2 61.8 %psum.63 = f32[16,32]{1,0:T(8,128)S(1)} all-reduce(f32[16,32]{1,0:T(8,128)S(1)} %psum.62), channel_id=1, replica_groups=mesh['row'=16,'col'=32] {'col'}, use_global_device_ids=true, to_apply=%region_9.10 | all-reduce | flops 512 | bytes 4096 | tf_op jit(solution)/shard_map/psum | solution.py:116
  761.3 5.4 fusion.29
  766.7 138.2 %all-reduce.9.cloned.1.call-done = f32[16,32,32]{1,2,0:T(8,128)} async-done(((f32[16,32,32]{1,2,0:T(8,128)}), f32[16,32,32]{1,2,0:T(8,128)}) %all-reduce.9.cloned.1.call-update) | async-done | bytes 65552 | tf_op jit(solution)/shard_map/psum | solution.py:116
  905.0 290.2 %all-reduce.11.cloned.1.call-done = f32[16,32,32]{1,2,0:T(8,128)} async-done(((f32[16,32,32]{1,2,0:T(8,128)}), f32[16,32,32]{1,2,0:T(8,128)}) %all-reduce.11.cloned.1.call-update) | async-done | bytes 65552 | tf_op jit(solution)/shard_map/psum | solution.py:116
  1195.1 6.1 fusion
  1201.3 1.0 copy.31
  1202.3 1.0 reshape.56
  1203.6 22.5 %collective-permute-start.16 = (bf16[1,32,256]{2,1,0:T(8,128)(2,1)S(1)}, bf16[1,32,256]{2,1,0:T(8,128)(2,1)S(1)}, u32[]{:S(2)}, u32[]{:S(2)}) collective-permute-start(bf16[1,32,256]{2,1,0:T(8,128)(2,1)S(1)} %get-tuple-element.86), channel_id=1, source_target_pairs={{0,32},{32,64},{64,96},{96,128},{128,160},{160,192},{192,224},{224... | collective-permute-start | bytes 49160 | tf_op jit(solution)/shard_map/ppermute | solution.py:17
  1226.1 1.9 collective-permute-start.17
  1228.2 2.9 collective-permute-done.17
  1231.2 3.1 collective-permute-start.18
  1234.3 1.3 collective-permute-start.19
  1235.9 4.2 collective-permute-done.19
  (159 shorter events, 13.8 us)
Async XLA Ops:
  7.2 13.1 %copy-start.35 = (f32[2,256]{1,0:T(2,128)S(1)}, f32[2,256]{1,0:T(2,128)}, u32[]{:S(2)}) copy-start(f32[2,256]{1,0:T(2,128)} %param.20) | copy-start | bytes 6148
  7.2 13.7 %copy-start.32 = (f32[2,1024]{1,0:T(2,128)S(1)}, f32[2,1024]{1,0:T(2,128)}, u32[]{:S(2)}) copy-start(f32[2,1024]{1,0:T(2,128)} %param.18) | copy-start | bytes 24580
  7.2 14.3 %copy-start.14 = (f32[2,3,3,1024]{3,0,2,1:T(2,128)S(1)}, f32[2,3,3,1024]{3,0,2,1:T(2,128)}, u32[]{:S(2)}) copy-start(f32[2,3,3,1024]{3,0,2,1:T(2,128)} %param.17) | copy-start | bytes 221188
  7.2 14.4 %copy-start.9 = (f32[2,5,5,768]{3,0,2,1:T(2,128)S(1)}, f32[2,5,5,768]{3,0,2,1:T(2,128)}, u32[]{:S(2)}) copy-start(f32[2,5,5,768]{3,0,2,1:T(2,128)} %param.22) | copy-start | bytes 460804
  7.2 295.8 %all-reduce.5.cloned.1.call-start = ((), (), s32[]{:S(2)}) async-start(), calls=%async_computation | async-start | bytes 524288 | tf_op jit(solution)/shard_map/psum | solution.py:116
  8.6 13.8 %copy-start.36 = (f32[2,256]{1,0:T(2,128)S(1)}, f32[2,256]{1,0:T(2,128)}, u32[]{:S(2)}) copy-start(f32[2,256]{1,0:T(2,128)} %param.25) | copy-start | bytes 6148
  10.1 12.8 %collective-permute-start = (bf16[1,32,1024]{2,1,0:T(8,128)(2,1)S(1)}, bf16[1,32,1024]{2,1,0:T(8,128)(2,1)S(1)}, u32[]{:S(2)}, u32[]{:S(2)}) collective-permute-start(bf16[1,32,1024]{2,1,0:T(8,128)(2,1)S(1)} %get-tuple-element.74), channel_id=1, source_target_pairs={{0,32},{32,64},{64,96},{96,128},{128,160},{160,192},{192,224},{224... | collective-permute-start | bytes 196616 | tf_op jit(solution)/shard_map/ppermute | solution.py:17
  14.7 8.2 collective-permute-start.1
  23.0 8.6 copy-start.42
  23.0 8.6 copy-start.45
  23.1 3.9 collective-permute-start.2
  24.9 6.3 collective-permute-start.3
  33.1 6.6 copy-start.10
  34.1 7.9 collective-permute-start.4
  37.8 6.1 collective-permute-start.5
  44.0 9.3 collective-permute-start.6
  50.0 6.2 collective-permute-start.7
  53.2 3.3 copy-start.15
  53.2 3.3 copy-start.16
  53.2 3.3 copy-start.17
  53.2 3.4 copy-start.18
  53.2 3.4 copy-start.19
  53.2 3.4 copy-start.20
  53.2 3.4 copy-start.21
  53.2 3.4 copy-start.22
  53.2 3.4 copy-start.23
  53.2 3.4 copy-start.24
  53.3 3.4 copy-start.25
  53.3 3.4 copy-start.26
  53.3 3.4 copy-start.27
  53.3 3.4 copy-start.28
  53.3 3.4 copy-start.29
  53.3 3.4 copy-start.30
  53.3 3.4 copy-start.31
  161.1 432.3 %all-reduce.7.cloned.1.call-start = ((), (), s32[]{:S(2)}) async-start(), calls=%async_computation.1 | async-start | bytes 524288 | tf_op jit(solution)/shard_map/psum | solution.py:116
  303.1 601.9 %all-reduce.9.cloned.1.call-start = ((), (), s32[]{:S(2)}) async-start(), calls=%async_computation.2 | async-start | bytes 524288 | tf_op jit(solution)/shard_map/psum | solution.py:116
  599.5 2.0 copy-start.11
  599.5 2.0 copy-start.39
  599.5 3.2 copy-start.34
  600.5 2.2 copy-start.41
  602.8 32.9 %copy-start.8 = (f32[5,5,768]{2,1,0:T(8,128)S(1)}, f32[5,5,768]{2,1,0:T(8,128)}, u32[]{:S(2)}) copy-start(f32[5,5,768]{2,1,0:T(8,128)} %get-tuple-element.118) | copy-start | bytes 230404
  603.2 24.5 %collective-permute-start.8 = (bf16[1,32,1024]{2,1,0:T(8,128)(2,1)S(1)}, bf16[1,32,1024]{2,1,0:T(8,128)(2,1)S(1)}, u32[]{:S(2)}, u32[]{:S(2)}) collective-permute-start(bf16[1,32,1024]{2,1,0:T(8,128)(2,1)S(1)} %get-tuple-element.72), channel_id=1, source_target_pairs={{0,32},{32,64},{64,96},{96,128},{128,160},{160,192},{192,224},{224... | collective-permute-start | bytes 196616 | tf_op jit(solution)/shard_map/ppermute | solution.py:17
  625.7 5.6 collective-permute-start.9
  627.7 13.4 %copy-start.33 = (f32[1,1024]{1,0:T(1,128)S(1)}, f32[1,1024]{1,0:T(1,128)}, u32[]{:S(2)}) copy-start(f32[1,1024]{1,0:T(1,128)} %get-tuple-element.108) | copy-start | bytes 12292
  627.7 13.4 %copy-start.38 = (f32[1,256]{1,0:T(1,128)S(1)}, f32[1,256]{1,0:T(1,128)}, u32[]{:S(2)}) copy-start(f32[1,256]{1,0:T(1,128)} %get-tuple-element.114) | copy-start | bytes 3076
  627.7 13.4 %copy-start.43 = (bf16[2,1024,256]{2,1,0:T(8,128)(2,1)S(1)}, bf16[2,1024,256]{2,1,0:T(8,128)(2,1)}, u32[]{:S(2)}) copy-start(bf16[2,1024,256]{2,1,0:T(8,128)(2,1)} %param.19) | copy-start | bytes 3145732
  631.4 4.5 collective-permute-start.10
  634.4 6.3 collective-permute-start.11
  642.6 5.0 copy-start.12
  642.9 6.3 collective-permute-start.12
  645.6 5.9 collective-permute-start.13
  651.6 8.9 collective-permute-start.14
  657.1 6.2 collective-permute-start.15
  761.0 434.1 %all-reduce.11.cloned.1.call-start = ((), (), s32[]{:S(2)}) async-start(), calls=%async_computation.3 | async-start | bytes 524288 | tf_op jit(solution)/shard_map/psum | solution.py:116
  1201.3 2.0 copy-start.13
  1201.3 2.0 copy-start.37
  1201.3 2.0 copy-start.44
  1201.3 26.7 %copy-start.40 = (bf16[3,3,4,256]{3,2,1,0:T(4,128)(2,1)S(1)}, bf16[3,3,4,256]{3,2,1,0:T(4,128)(2,1)}, u32[]{:S(2)}) copy-start(bf16[3,3,4,256]{3,2,1,0:T(4,128)(2,1)} %param.26) | copy-start | bytes 55300
  1203.3 37.9 %copy-start.46 = (f32[4]{0:T(128)S(1)}, f32[4]{0:T(128)}, u32[]{:S(2)}) copy-start(f32[4]{0:T(128)} %param.27) | copy-start | bytes 52
  1203.6 38.5 %copy-start.4 = (bf16[8,32,256]{2,1,0:T(8,128)(2,1)}, bf16[8,32,256]{2,1,0:T(8,128)(2,1)S(1)}, u32[]{:S(2)}) copy-start(bf16[8,32,256]{2,1,0:T(8,128)(2,1)S(1)} %fusion.9) | copy-start | bytes 393220
  1203.6 24.6 %collective-permute-start.16 = (bf16[1,32,256]{2,1,0:T(8,128)(2,1)S(1)}, bf16[1,32,256]{2,1,0:T(8,128)(2,1)S(1)}, u32[]{:S(2)}, u32[]{:S(2)}) collective-permute-start(bf16[1,32,256]{2,1,0:T(8,128)(2,1)S(1)} %get-tuple-element.86), channel_id=1, source_target_pairs={{0,32},{32,64},{64,96},{96,128},{128,160},{160,192},{192,224},{224... | collective-permute-start | bytes 49160 | tf_op jit(solution)/shard_map/ppermute | solution.py:17
  1226.1 5.1 collective-permute-start.17
  1231.2 4.8 collective-permute-start.18
  1234.3 5.9 collective-permute-start.19
  (7 other events, 10.8 us)
Sparse Core Ops, SparseCore 0:
  161.2 141.8 all-reduce.4
  306.2 287.1 all-reduce.6
  761.1 143.7 all-reduce.8
  907.9 287.1 all-reduce.10
